TPU v7x, 32 devices: a whole 2x2x4 slice. The times are simulated.
32 devices in a mesh: groups: 1, gcol: 16 (over z, y, x), grow: 2 (over core).
Axes of the slice: x: 2, y: 2, z: 4, core: 2. Of those that a mesh axis runs over, the one named last changes fastest.
Arguments:
- ancestor_inverse: bfloat16 [6144, 6144], P(('groups', 'gcol')), may hold values from -6 to 6
- lower_rows: bfloat16 [2, 4096, 1024], P('groups', 'gcol'), may hold values from -0.09375 to 0.09375
- factor_inverse: bfloat16 [2, 1024, 1024], P('groups', 'gcol'), may hold values from -0.1875 to 0.1875
- block_lists: int32 [2, 32], P('groups'), may hold values from 0 to 47, as said below
- live_counts: int32 [2], P('groups'), may hold values from 16 to 32, as said below
Outputs:
- ancestor_columns: bfloat16 [2, 6144, 1024], P('groups', 'gcol', 'grow')
- diagonal_inverse: float32 [2, 2, 512, 1024], P('groups', 'grow', 'gcol')
Inputs may be any that keep to these rules, and one draw needn't show every extreme that they name: `live_counts`: supernode 0 uses all 32 slots; the other supernodes use at least half of them. `block_lists`: in each supernode all entries are distinct; the live slots come first in increasing order of pool block.
All inputs are finite; a program needn't handle non-finite values.
Results may differ from a plain program's by a relative error of at most 0.0057.
Values may be sent and summed in bfloat16 or wider, within the bound.
A program may use at most 128 MiB of HBM per device.

v0:
```python
import jax
import jax.numpy as jnp
from jax import lax
from jax.sharding import PartitionSpec as P

BLK = 128


def swapped(block, axis, bit):
    count = lax.axis_size(axis)
    route = []
    for low in range(count):
        high = low | 1 << bit
        if high != low and high < count:
            route += [(low, high), (high, low)]
    return lax.ppermute(block, axis, route)


def slot_folder(selected, wanted, totals, portion):
    product_acc, picked = totals
    amount = portion.shape[1]
    product_acc = jnp.einsum("sqj,sjh->sqh", selected, portion, preferred_element_type=jnp.float32)
    inside = (wanted >= 0) & (wanted < amount)
    taken = jnp.take_along_axis(portion, jnp.clip(wanted, 0, amount - 1)[:, :, None], axis=1)
    picked = jnp.where(inside[:, :, None], taken, picked)
    return (product_acc, picked)


def shards(ancestor_inverse, lower_rows, factor_inverse, block_lists, live_counts):
    supernodes, slot_rows, order_size = lower_rows.shape
    own_rows, pool_width = ancestor_inverse.shape
    column = lax.axis_index("gcol")
    parity = lax.axis_index("grow")
    half_width = order_size // lax.axis_size("grow")
    out_rows = half_width // lax.axis_size("gcol")
    slot_total = block_lists.shape[1]
    own_blocks = own_rows // BLK
    pool_blocks = pool_width // BLK
    slot_dev = slot_rows // BLK
    half_start = parity * half_width
    row_start = half_start + column * out_rows
    portion = lax.all_gather(factor_inverse, "gcol", axis=1, tiled=True)
    factor_part = lax.dynamic_slice_in_dim(portion, half_start, half_width, 2)
    own_part = lax.dynamic_slice_in_dim(portion, row_start, out_rows, 2)
    scaled_acc = jnp.einsum(
        "smk,skn->smn", lower_rows, factor_part, preferred_element_type=jnp.float32
    )
    own_acc = jnp.einsum("ska,skb->sab", own_part, portion, preferred_element_type=jnp.float32)
    scaled_acc, own_acc = (scaled_acc, own_acc)
    slot_ids = column * slot_dev + jnp.arange(slot_dev, dtype=jnp.int32)
    slot_live = slot_ids[None, :] < live_counts[:, None]
    row_live = jnp.repeat(slot_live, BLK, axis=1)
    scaled = jnp.where(row_live[:, :, None], scaled_acc, 0.0).astype(jnp.bfloat16)
    block_ids = column * own_blocks + jnp.arange(own_blocks, dtype=jnp.int32)
    all_live = jnp.arange(slot_total, dtype=jnp.int32)[None, :] < live_counts[:, None]
    matches = (block_lists[:, None, :] == block_ids[None, :, None]) & all_live[:, None, :]
    member = jnp.any(matches, axis=2)
    slot_of = jnp.sum(
        jnp.where(matches, jnp.arange(slot_total, dtype=jnp.int32)[None, None, :], 0), axis=2
    )
    member_rows = jnp.repeat(member, BLK, axis=1)
    wanted = (slot_of[:, :, None] * BLK + jnp.arange(BLK, dtype=jnp.int32)[None, None, :]).reshape(
        supernodes, own_rows
    )
    blocked = ancestor_inverse.reshape(own_rows, pool_blocks, BLK)
    selected = jnp.transpose(jnp.take(blocked, block_lists, axis=1), (1, 0, 2, 3)).reshape(
        supernodes, own_rows, slot_total * BLK
    )
    start_state = (
        jnp.zeros((supernodes, own_rows, half_width), jnp.float32),
        jnp.zeros((supernodes, own_rows, half_width), jnp.bfloat16),
    )
    product_acc, picked = slot_folder(
        selected, wanted, start_state, lax.all_gather(scaled, "gcol", axis=1, tiled=True)
    )
    ancestor = jnp.where(member_rows[:, :, None], -product_acc, 0.0).astype(jnp.bfloat16)
    partner = swapped(ancestor, "grow", 0)
    lower_half = jnp.where(parity == 0, ancestor, partner)
    second = jnp.where(parity == 0, partner, ancestor)
    ancestor_full = jnp.concatenate([lower_half, second], axis=2)
    term = jnp.einsum("sqa,sqb->asb", picked, ancestor_full, preferred_element_type=jnp.float32)
    shared = lax.psum_scatter(term, "gcol", scatter_dimension=0, tiled=True)
    diagonal = own_acc - jnp.transpose(shared, (1, 0, 2))
    return (ancestor, diagonal[:, None, :, :])


def solution(mesh):
    return jax.shard_map(
        shards,
        mesh=mesh,
        in_specs=(
            P(("groups", "gcol"), None),
            P("groups", "gcol", None),
            P("groups", "gcol", None),
            P("groups", None),
            P("groups"),
        ),
        out_specs=(P("groups", "gcol", "grow"), P("groups", "grow", "gcol", None)),
        check_vma=False,
    )
```

profile of v0, /device:TPU:0, one launch (start us, length us, event | category | flops | bytes accessed | tf_op | source)
XLA Modules:
  0.0 363.2 jit_solution(29231205271821577)
XLA Ops:
  7.2 0.0 copy-start
  7.2 0.0 all-gather.3.cloned.1.call-start
  7.2 2.0 copy.49
  9.2 0.0 all-gather.3.cloned.1.call-update
  9.3 0.0 all-gather.5.cloned.1.call-start
  9.3 0.7 broadcast_compare_fusion
  10.0 0.1 broadcast_bitcast_fusion.1
  10.1 0.0 copy-start.3
  10.1 0.0 copy-start.2
  10.1 80.0 %all-gather.3.cloned.1.call-done = bf16[2,1024,1024]{2,0,1:T(2,128)(2,1)} async-done(((bf16[2,64,1024]{2,0,1:T(2,128)(2,1)}), bf16[2,1024,1024]{2,0,1:T(2,128)(2,1)}) %all-gather.3.cloned.1.call-update) | async-done | bytes 4194320 | tf_op jit(solution)/shard_map/all_gather | solution.py:42
  90.2 3.0 constant_dynamic-slice_fusion.1
  93.2 0.0 copy-done
  93.2 1.7 fusion.18
  94.9 0.0 all-gather.5.cloned.1.call-update
  95.0 0.2 reduce-scatter.2.cloned.1.call-start
  95.2 0.0 copy-done.3
  95.2 0.1 iota_compare_fusion
  95.3 0.0 copy-done.2
  95.3 0.2 fusion.30
  95.5 0.1 copy.62
  95.6 0.1 broadcast_bitcast_fusion.2
  95.7 0.1 reshape.138
  95.8 6.7 %copy.46 = bf16[384,6144]{0,1:T(8,128)(2,1)} copy(bf16[384,6144]{1,0:T(8,128)(2,1)} %param.5) | data formatting | bytes 9437184 | tf_op args[0]
  102.5 6.7 %copy.47 = bf16[384,48,128]{2,0,1:T(8,128)(2,1)} copy(bf16[384,48,128]{0,2,1:T(8,128)(2,1)} %bitcast.49) | data formatting | bytes 9437184 | tf_op jit(solution)/shard_map/reshape | solution.py:65
  109.2 6.4 %gather_fusion = bf16[64,384,128]{2,1,0:T(8,128)(2,1)} fusion(bf16[384,48,128]{2,0,1:T(8,128)(2,1)} %copy.47, s32[1024]{0:T(1024)S(1)} %pad_clamp_fusion), kind=kCustom, calls=%fused_computation | custom fusion | bytes 12583168 | tf_op jit(solution)/shard_map/jit(_take)/gather | solution.py:66
  115.5 0.2 fusion.31
  115.8 113.2 %all-gather.5.cloned.1.call-done = bf16[2,4096,512]{1,2,0:T(8,128)(2,1)} async-done(((bf16[2,256,512]{1,2,0:T(8,128)(2,1)}), bf16[2,4096,512]{1,2,0:T(8,128)(2,1)}) %all-gather.5.cloned.1.call-update) | async-done | bytes 8388624 | tf_op jit(solution)/shard_map/all_gather | solution.py:74
  229.0 8.6 %select_convert_fusion = bf16[2,384,512]{2,1,0:T(8,128)(2,1)S(1)} fusion(bf16[2,4096,512]{1,2,0:T(8,128)(2,1)} %all-gather.5.cloned.1.call-done, pred[2,384]{1,0:T(4,128)(4,1)S(1)} %bitcast.52, bf16[2,32,384,128]{3,2,1,0:T(8,128)(2,1)} %bitcast.50, pred[2,32]{1,0:T(4,128)(4,1)S(1)} %compare_and_fusion.3), kind=kOutput, calls=%fused_computation.14 | convolution fusion | flops 3225550848 | bytes 15467328 | tf_op jit(solution)/shard_map/sqj,sjh->sqh/dot_general | solution.py:22
  237.6 0.0 copy-start.1
  237.6 0.1 collective-permute-start
  237.7 0.1 copy.54
  237.8 0.1 add.108
  237.9 0.1 broadcast_bitcast_fusion
  238.0 12.0 %copy.55 = bf16[2,4096,512]{2,1,0:T(8,128)(2,1)} copy(bf16[2,4096,512]{1,2,0:T(8,128)(2,1)} %all-gather.5.cloned.1.call-done) | data formatting | bytes 16777216 | tf_op jit(solution)/shard_map/all_gather | solution.py:74
  250.0 8.2 %gather_fusion.1 = bf16[768,512]{1,0:T(8,128)(2,1)S(1)} fusion(bf16[2,4096,512]{2,1,0:T(8,128)(2,1)} %copy.55, s32[768]{0:T(1024)S(1)} %reshape.144), kind=kCustom, calls=%fused_computation.1 | custom fusion | bytes 1579008 | tf_op jit(solution)/shard_map/jit(take_along_axis)/gather | solution.py:24
  258.2 0.0 collective-permute-done
  258.2 0.0 copy-done.1
  258.2 0.1 broadcast_select_fusion.1
  258.3 3.1 convolution_bitcast_fusion
  261.4 0.0 reduce-scatter.2.cloned.1.call-update
  261.4 1.7 constant_dynamic-slice_fusion
  263.1 3.6 fusion.3
  266.7 88.3 %reduce-scatter.2.cloned.1.call-done = f32[32,2,1024]{2,0,1:T(8,128)} async-done(((f32[512,2,1024]{2,0,1:T(8,128)}), f32[32,2,1024]{2,0,1:T(8,128)}) %reduce-scatter.2.cloned.1.call-update) | async-done | bytes 262160 | tf_op jit(solution)/shard_map/reduce_scatter | solution.py:82
  355.0 1.7 fusion.28
  (13 shorter events, 0.1 us)
Async XLA Ops:
  7.2 86.0 %copy-start = (bf16[2,256,1024]{2,1,0:T(8,128)(2,1)S(1)}, bf16[2,256,1024]{2,1,0:T(8,128)(2,1)}, u32[]{:S(2)}) copy-start(bf16[2,256,1024]{2,1,0:T(8,128)(2,1)} %param.6) | copy-start | bytes 3145732
  7.2 83.0 %all-gather.3.cloned.1.call-start = ((), (), s32[]{:S(2)}) async-start(), calls=%async_computation.1 | async-start | bytes 4456448 | tf_op jit(solution)/shard_map/all_gather | solution.py:42
  9.3 219.7 %all-gather.5.cloned.1.call-start = ((), (), s32[]{:S(2)}) async-start(), calls=%async_computation.2 | async-start | bytes 8912896 | tf_op jit(solution)/shard_map/all_gather | solution.py:74
  10.1 85.1 %copy-start.3 = (s32[2]{0:T(128)S(1)}, s32[2]{0:T(128)}, u32[]{:S(2)}) copy-start(s32[2]{0:T(128)} %param.9) | copy-start | bytes 28
  10.1 85.2 %copy-start.2 = (s32[2,32]{1,0:T(2,128)S(1)}, s32[2,32]{1,0:T(2,128)}, u32[]{:S(2)}) copy-start(s32[2,32]{1,0:T(2,128)} %param.8) | copy-start | bytes 772
  95.0 260.0 %reduce-scatter.2.cloned.1.call-start = ((), (), s32[]{:S(2)}) async-start(), calls=%async_computation.3 | async-start | bytes 4456448 | tf_op jit(solution)/shard_map/reduce_scatter | solution.py:82
  237.6 20.6 %copy-start.1 = (bf16[2,384,512]{2,1,0:T(8,128)(2,1)}, bf16[2,384,512]{2,1,0:T(8,128)(2,1)S(1)}, u32[]{:S(2)}) copy-start(bf16[2,384,512]{2,1,0:T(8,128)(2,1)S(1)} %select_convert_fusion) | copy-start | bytes 2359300
  237.6 20.6 %collective-permute-start = (bf16[2,384,512]{2,1,0:T(8,128)(2,1)S(1)}, bf16[2,384,512]{2,1,0:T(8,128)(2,1)S(1)}, u32[]{:S(2)}, u32[]{:S(2)}) collective-permute-start(bf16[2,384,512]{2,1,0:T(8,128)(2,1)S(1)} %select_convert_fusion), channel_id=1, source_target_pairs={{0,1},{1,0},{2,3},{3,2},{4,5},{5,4},{6,7},{7,6},{8,9},{9,8},{10,11... | collective-permute-start | bytes 2359304 | tf_op jit(solution)/shard_map/ppermute | solution.py:16
Sparse Core Ops, SparseCore 0:
  11.4 78.7 all-gather.2
  95.1 133.8 all-gather.4
  261.5 93.4 reduce-scatter.1
where the time goes:
time: 364 us; the launch traced here: 363 us
  waiting for transfers between devices  282 us (77%)
  local copies, waits for them, and re-layouts  47.2 us (13%)
  matrix products  17 us (5%)
  between operations  13.9 us (4%)
    all_gather x1, waiting for transfers between devices, shards(): lax.all_gather(scaled, 'gcol', axis=1, tiled=True)  113 us
    reduce_scatter x1, waiting for transfers between devices, shards(): shared = lax.psum_scatter(term, 'gcol', scatter_dimension=0, tiled=True)  88.3 us
    all_gather x1, waiting for transfers between devices, shards(): portion = lax.all_gather(factor_inverse, 'gcol', axis=1, tiled=True)  80 us
    all_gather x1, local copies, waits for them, and re-layouts, shards(): lax.all_gather(scaled, 'gcol', axis=1, tiled=True)  12 us
    unnamed x16, local copies, waits for them, and re-layouts  9.08 us
    dot_general x1, matrix products, slot_folder(): jnp.einsum('sqj,sjh->sqh', selected, portion, preferred_element_type=jnp....  8.65 us
    gather x2, local copies, waits for them, and re-layouts, slot_folder(): jnp.take_along_axis(portion, jnp.clip(wanted, 0, amount - 1)[:, :, None],...  8.18 us
  transfers between devices with their start and end apart: 4, of which 3 were waited for; matrix products, arithmetic and copies ran while one was open for 13% of the time, Pallas kernels for 0%

commit v1 on v0

v1 whole, which is shorter than its diff:
```python
import functools

import jax
import jax.numpy as jnp
from jax import lax
from jax.experimental import pallas as pl
from jax.experimental.pallas import tpu as pltpu
from jax.sharding import PartitionSpec as P

BLK = 128
MESH = pl.DeviceIdType.MESH
F32 = jnp.float32
BF16 = jnp.bfloat16


def guarded(pred, action):
    if pred is None:
        action()
    else:
        pl.when(pred)(action)


class Net:
    def __init__(self, send_sems, recv_sems):
        self.send_sems, self.recv_sems = send_sems, recv_sems
        self.used = 0
        self.pending = []

    def take(self, count):
        base = self.used
        self.used += count
        return base

    def push(self, src, dst, send, recv, device, pred=None):
        def copy():
            return pltpu.make_async_remote_copy(
                src_ref=src,
                dst_ref=dst,
                send_sem=self.send_sems.at[send],
                recv_sem=self.recv_sems.at[recv],
                device_id=device,
                device_id_type=MESH,
            )

        guarded(pred, lambda: copy().start())
        self.pending.append((pred, copy))

    def arrived(self, dst, recv, device, pred=None):
        def wait():
            pltpu.make_async_remote_copy(
                src_ref=dst,
                dst_ref=dst,
                send_sem=self.send_sems.at[recv],
                recv_sem=self.recv_sems.at[recv],
                device_id=device,
                device_id_type=MESH,
            ).wait_recv()

        guarded(pred, wait)

    def drain(self):
        for pred, copy in self.pending:
            guarded(pred, lambda copy=copy: copy().wait_send())


def run(tasks):
    active = list(tasks)
    while active:
        for task in list(active):
            try:
                next(task)
            except StopIteration:
                active.remove(task)


def together(tasks):
    active = list(tasks)
    while active:
        for task in list(active):
            try:
                next(task)
            except StopIteration:
                active.remove(task)
        yield


def gather(net, view, order, pos, sizes, peer):
    z, planes = pos["z"], sizes["z"]

    def region(zs, done, flip=None):
        index = {}
        for axis in "yx":
            if axis in done:
                index[axis] = slice(None)
            else:
                index[axis] = 1 - pos[axis] if axis == flip else pos[axis]
        return view(zs, index["y"], index["x"])

    place = order.index("z")
    before = [axis for axis in order[:place] if sizes[axis] > 1]
    after = [axis for axis in order[place + 1 :] if sizes[axis] > 1]
    done = set()
    for axis in before:
        sem = net.take(1)
        mine = region(z, done)
        net.push(mine, mine, sem, sem, peer(axis))
        yield
        net.arrived(region(z, done, axis), sem, peer(axis))
        done = done | {axis}
    bases = {axis: net.take(planes) for axis in after}
    up, down = net.take(planes), net.take(planes)

    def forward(axis, zs, finished, pred):
        piece = region(zs, finished)
        net.push(piece, piece, bases[axis] + zs, bases[axis] + zs, peer(axis), pred)

    for k in range(planes - 1):
        lower, upper = z - k, z + k
        piece = region(lower, done)
        net.push(piece, piece, up + lower, up + lower, peer("z", z + 1), (z < planes - 1) & (lower >= 0))
        piece = region(upper, done)
        net.push(piece, piece, down + upper, down + upper, peer("z", z - 1), (z > 0) & (upper < planes))
        if k == 0 and after:
            forward(after[0], z, done, None)
        yield
        lower, upper = lower - 1, upper + 1
        net.arrived(region(lower, done), up + lower, peer("z", z - 1), lower >= 0)
        if after:
            forward(after[0], lower, done, lower >= 0)
        net.arrived(region(upper, done), down + upper, peer("z", z + 1), upper < planes)
        if after:
            forward(after[0], upper, done, upper < planes)
    for i, axis in enumerate(after):
        for far in range(planes):
            yield
            for zs, pred in [(z, None)] if far == 0 else [(z - far, z >= far), (z + far, z + far < planes)]:
                net.arrived(region(zs, done, axis), bases[axis] + zs, peer(axis), pred)
                if i + 1 < len(after):
                    forward(after[i + 1], zs, done | {axis}, pred)
        done = done | {axis}


def kernel(
    sizes, live_ref, hit_ref, factor_ref, lower_ref, chosen_hbm, anc_ref, diag_ref,
    chosen, fbuf, sbufs, acc, picked_acc, own_neg, other_neg, terms, kept,
    send_a, recv_a, send_b, recv_b, send_c, recv_c, send_sems, recv_sems, chosen_sem,
):
    nz, ny, nx = sizes["z"], sizes["y"], sizes["x"]
    supernodes, piece_rows, order_size = factor_ref.shape
    slot_rows = lower_ref.shape[1]
    slot_dev = slot_rows // BLK
    slot_total = hit_ref.shape[2]
    own_rows = chosen_hbm.shape[1]
    own_blocks = own_rows // BLK
    half = order_size // 2
    out_rows = diag_ref.shape[1]
    column = lax.axis_index("gcol")
    parity = lax.axis_index("grow")
    x = column % nx
    y = (column // nx) % ny
    z = column // (nx * ny)
    pos = {"z": z, "y": y, "x": x}
    own_cols = pl.ds(pl.multiple_of(parity * half, half), half)
    other_cols = pl.ds(pl.multiple_of((1 - parity) * half, half), half)
    mate = {"grow": 1 - parity}

    def peer(axis, to=None):
        if axis == "x":
            return {"gcol": (z * ny + y) * nx + 1 - x}
        if axis == "y":
            return {"gcol": (z * ny + 1 - y) * nx + x}
        return {"gcol": (to * ny + y) * nx + x}

    chosen_copy = pltpu.make_async_copy(chosen_hbm, chosen, chosen_sem)
    chosen_copy.start()
    barrier = pltpu.get_barrier_semaphore()
    greeted = [mate] + [peer(axis) for axis in "xy" if sizes[axis] > 1]
    greeted += [peer("z", (z + d) % nz) for d in range(1, nz)]
    for device in greeted:
        pl.semaphore_signal(barrier, inc=1, device_id=device, device_id_type=MESH)
    for s in range(supernodes):
        fbuf[s, z, y, x] = factor_ref[s, :, own_cols]
    members = [
        [sum(hit_ref[s, b, j] for j in range(slot_total)) for b in range(own_blocks)] for s in range(supernodes)
    ]
    pl.semaphore_wait(barrier, len(greeted))

    net = Net(send_sems, recv_sems)
    orders = ["xzy", "yzx", "zxy", "zyx"] if nx * ny > 1 else ["zxy"]

    def gathers(make_view, rows):
        count = min(len(orders), rows // 16)
        step = rows // count
        return [
            gather(net, make_view(pl.ds(i * step, step)), orders[i], pos, sizes, peer) for i in range(count)
        ]

    run(gathers(lambda rows: lambda zs, ys, xs: fbuf.at[:, zs, ys, xs, rows, :], piece_rows))

    def scale(s):
        whole = fbuf[s].reshape(order_size, half)
        product = jnp.dot(lower_ref[s], whole, preferred_element_type=F32)
        for j in range(slot_dev):
            rows = slice(j * BLK, (j + 1) * BLK)
            sbufs[s][z, y, x, rows, :] = (product[rows] * live_ref[s, j]).astype(BF16)

    def scatter(s, u):
        first, second = ("x", "y") if u == 0 else ("y", "x")
        cols = own_cols if u == 0 else other_cols
        if nx * ny > 1:
            def part(one, two):
                index = {first: one, second: two}
                return terms[s, u, :, index["y"], index["x"]]

            a, b = pos[first], pos[second]
            for other in range(2):
                send_a[s, u, :, other] = part(1 - a, other).astype(BF16)
            sem = net.take(1)
            net.push(send_a.at[s, u], recv_a.at[s, u], sem, sem, peer(first))
            yield
            net.arrived(recv_a.at[s, u], sem, peer(first))
            send_b[s, u] = (part(a, 1 - b) + recv_a[s, u, :, 1 - b].astype(F32)).astype(BF16)
            sem = net.take(1)
            net.push(send_b.at[s, u], recv_b.at[s, u], sem, sem, peer(second))
            kept[s, u] = part(a, b) + recv_a[s, u, :, b].astype(F32)
            yield
            net.arrived(recv_b.at[s, u], sem, peer(second))
            kept[s, u] = kept[s, u] + recv_b[s, u].astype(F32)
        else:
            kept[s, u] = terms[s, u, :, 0, 0]
        send_c[s, u] = kept[s, u].astype(BF16)
        sem = net.take(nz)
        for d in range(1, nz):
            to = (z + d) % nz
            net.push(send_c.at[s, u, to], recv_c.at[s, u, d - 1], sem + d, sem + d, peer("z", to))
        yield
        total = kept[s, u, z]
        for d in range(1, nz):
            net.arrived(recv_c.at[s, u, d - 1], sem + d, peer("z", (z + d) % nz))
            total = total + recv_c[s, u, d - 1].astype(F32)
        diag_ref[s, :, cols] = total

    def finish(s):
        for plane in range(nz):
            width = ny * nx * slot_rows
            part = jnp.dot(
                chosen[s, :, plane * width : (plane + 1) * width],
                sbufs[s][plane].reshape(width, half),
                preferred_element_type=F32,
            )
            if plane == 0:
                acc[s] = part
            elif plane < nz - 1:
                acc[s] = acc[s] + part
            else:
                total = acc[s] + part
            for b in range(own_blocks):
                found = picked_acc[s, b] if plane > 0 else jnp.zeros((BLK, half), BF16)
                for i in range(ny * nx * slot_dev):
                    chip = i // slot_dev
                    rows = slice(i % slot_dev * BLK, (i % slot_dev + 1) * BLK)
                    weight = hit_ref[s, b, plane * ny * nx * slot_dev + i]
                    found += sbufs[s][plane, chip // nx, chip % nx, rows, :] * jnp.full((BLK, half), weight).astype(BF16)
                picked_acc[s, b] = found
            yield
        for b in range(own_blocks):
            rows = slice(b * BLK, (b + 1) * BLK)
            block = (total[rows] * members[s][b]).astype(BF16)
            own_neg[s, rows, :] = block
            anc_ref[s, rows, :] = -block
        sem = net.take(1)
        net.push(own_neg.at[s], other_neg.at[s], sem, sem, mate)
        left = jnp.concatenate([picked_acc[s].reshape(own_rows, half), factor_ref[s, :, own_cols]], axis=0)

        def term(u, neg, cols):
            right = jnp.concatenate([neg[s], factor_ref[s, :, cols]], axis=0)
            result = lax.dot_general(left, right, (((0,), (0,)), ((), ())), preferred_element_type=F32)
            terms[s, u] = result.reshape(nz, ny, nx, out_rows, half)

        term(0, own_neg, own_cols)
        lower_half = scatter(s, 0)
        next(lower_half)
        yield
        net.arrived(other_neg.at[s], sem, mate)
        term(1, other_neg, other_cols)
        yield from together([lower_half, scatter(s, 1)])

    def node(s):
        for _ in range(4 * s):
            yield
        scale(s)
        yield from together(
            gathers(lambda rows: lambda zs, ys, xs: sbufs[s].at[zs, ys, xs, rows, :], slot_rows)
        )
        if s == 0:
            chosen_copy.wait()
        yield from finish(s)

    run([node(s) for s in range(supernodes)])
    net.drain()


def choose(slot_dev, live_ref, list_ref, pool_hbm, chosen_hbm, live_out, hit_out, sems):
    column = lax.axis_index("gcol")
    supernodes, own_blocks, slot_total = hit_out.shape
    copies = []
    for s in range(supernodes):
        for j in range(slot_total):
            block = list_ref[s, j]
            copy = pltpu.make_async_copy(
                pool_hbm.at[:, pl.ds(pl.multiple_of(block * BLK, BLK), BLK)],
                chosen_hbm.at[s, :, pl.ds(j * BLK, BLK)],
                sems.at[s, j],
            )
            copy.start()
            copies.append(copy)
    for s in range(supernodes):
        live = live_ref[s]
        for j in range(slot_dev):
            live_out[s, j] = jnp.where(column * slot_dev + j < live, 1.0, 0.0)
        for j in range(slot_total):
            for b in range(own_blocks):
                match = (list_ref[s, j] == column * own_blocks + b) & (j < live)
                hit_out[s, b, j] = jnp.where(match, 1.0, 0.0)
    for copy in copies:
        copy.wait()


def shards(ancestor_inverse, lower_rows, factor_inverse, block_lists, live_counts):
    supernodes, slot_rows, order_size = lower_rows.shape
    own_rows = ancestor_inverse.shape[0]
    piece_rows = factor_inverse.shape[1]
    columns = lax.axis_size("gcol")
    side = 2 if lax.axis_size("groups") == 1 and columns % 4 == 0 else 1
    nz = columns // (side * side)
    sizes = {"z": nz, "y": side, "x": side}
    half = order_size // lax.axis_size("grow")
    out_rows = half // columns
    grid = (nz, side, side)
    sems = (1 + supernodes) * (4 if side > 1 else 1) * (4 * nz + 2) + supernodes * (1 + 2 * (2 + nz))
    slot_total = block_lists.shape[1]
    slot_dev = slot_rows // BLK
    chosen_shape = (supernodes, own_rows, slot_total * BLK)
    smem = pl.BlockSpec(memory_space=pltpu.SMEM)
    chosen, live, hit = pl.pallas_call(
        functools.partial(choose, slot_dev),
        out_shape=(
            jax.ShapeDtypeStruct(chosen_shape, BF16),
            jax.ShapeDtypeStruct((supernodes, slot_dev), F32),
            jax.ShapeDtypeStruct((supernodes, own_rows // BLK, slot_total), F32),
        ),
        in_specs=[smem, smem, pl.BlockSpec(memory_space=pl.ANY)],
        out_specs=(pl.BlockSpec(memory_space=pl.ANY), smem, smem),
        scratch_shapes=[pltpu.SemaphoreType.DMA((supernodes, slot_total))],
    )(live_counts, block_lists, ancestor_inverse)
    ancestor, diagonal = pl.pallas_call(
        functools.partial(kernel, sizes),
        out_shape=(
            jax.ShapeDtypeStruct((supernodes, own_rows, half), BF16),
            jax.ShapeDtypeStruct((supernodes, out_rows, order_size), F32),
        ),
        in_specs=[
            pl.BlockSpec(memory_space=pltpu.SMEM),
            pl.BlockSpec(memory_space=pltpu.SMEM),
            pl.BlockSpec(memory_space=pltpu.VMEM),
            pl.BlockSpec(memory_space=pltpu.VMEM),
            pl.BlockSpec(memory_space=pl.ANY),
        ],
        out_specs=(pl.BlockSpec(memory_space=pltpu.VMEM), pl.BlockSpec(memory_space=pltpu.VMEM)),
        scratch_shapes=[
            pltpu.VMEM(chosen_shape, BF16),
            pltpu.VMEM((supernodes,) + grid + (piece_rows, half), BF16),
            [pltpu.VMEM(grid + (slot_rows, half), BF16) for _ in range(supernodes)],
            pltpu.VMEM((supernodes, own_rows, half), F32),
            pltpu.VMEM((supernodes, own_rows // BLK, BLK, half), BF16),
            pltpu.VMEM((supernodes, own_rows, half), BF16),
            pltpu.VMEM((supernodes, own_rows, half), BF16),
            pltpu.VMEM((supernodes, 2) + grid + (out_rows, half), F32),
            pltpu.VMEM((supernodes, 2, nz, out_rows, half), F32),
            pltpu.VMEM((supernodes, 2, nz, side, out_rows, half), BF16),
            pltpu.VMEM((supernodes, 2, nz, side, out_rows, half), BF16),
            pltpu.VMEM((supernodes, 2, nz, out_rows, half), BF16),
            pltpu.VMEM((supernodes, 2, nz, out_rows, half), BF16),
            pltpu.VMEM((supernodes, 2, nz, out_rows, half), BF16),
            pltpu.VMEM((supernodes, 2, nz, out_rows, half), BF16),
            pltpu.SemaphoreType.DMA((sems,)),
            pltpu.SemaphoreType.DMA((sems,)),
            pltpu.SemaphoreType.DMA,
        ],
        compiler_params=pltpu.CompilerParams(
            collective_id=0, has_side_effects=True, vmem_limit_bytes=58 * 1024 * 1024
        ),
    )(live, hit, factor_inverse, lower_rows, chosen)
    return (ancestor, diagonal[:, None, :, :])


def solution(mesh):
    return jax.shard_map(
        shards,
        mesh=mesh,
        in_specs=(
            P(("groups", "gcol"), None),
            P("groups", "gcol", None),
            P("groups", "gcol", None),
            P("groups", None),
            P("groups"),
        ),
        out_specs=(P("groups", "gcol", "grow"), P("groups", "grow", "gcol", None)),
        check_vma=False,
    )
```

time: 364 us -> 343 us (0.942)
  Pallas kernels: 0 us -> 338 us
  waiting for transfers between devices: 282 us -> 0 us
  local copies, waits for them, and re-layouts: 47.2 us -> 3.73 us
  matrix products: 17 us -> 0 us
  between operations: 13.9 us -> 0.65 us
    pallas_call x0 -> x2, Pallas kernels: none -> 338 us  [the longest x1 194 us: shards(): pl.pallas_call(functools.partial(choose, slot_dev), out_shape=(jax.ShapeD...]
    all_gather x2 -> x0, waiting for transfers between devices: 193 us -> none  [the longest x1 113 us: shards(): lax.all_gather(scaled, 'gcol', axis=1, tiled=True)]
    reduce_scatter x1 -> x0, waiting for transfers between devices: 88.3 us -> none  [shards(): shared = lax.psum_scatter(term, 'gcol', scatter_dimension=0, tiled=True)]
    dot_general x4 -> x0, matrix products: 17 us -> none  [the longest x1 8.65 us: slot_folder(): jnp.einsum('sqj,sjh->sqh', selected, portion, preferred_element_type=jnp....]
    gather x3 -> x0, local copies, waits for them, and re-layouts: 14.6 us -> none  [the longest x2 8.18 us: slot_folder(): jnp.take_along_axis(portion, jnp.clip(wanted, 0, amount - 1)[:, :, None],...]
    all_gather x1 -> x0, local copies, waits for them, and re-layouts: 12 us -> none  [shards(): lax.all_gather(scaled, 'gcol', axis=1, tiled=True)]
    reshape x1 -> x0, local copies, waits for them, and re-layouts: 6.65 us -> none  [shards(): blocked = ancestor_inverse.reshape(own_rows, pool_blocks, BLK)]
    unnamed x16 -> x2, local copies, waits for them, and re-layouts: 9.08 us -> 3.73 us
  transfers between devices with their start and end apart: 4 -> 0, of which waited for: 3 -> 0; matrix products, arithmetic and copies ran while one was open for 13% -> 0% of each run, Pallas kernels for 0% -> 0%
where the time goes in v1:
time: 343 us
  Pallas kernels  338 us (99%)
  local copies, waits for them, and re-layouts  3.73 us (1%)
    pallas_call x1, Pallas kernels, shards(): pl.pallas_call(functools.partial(choose, slot_dev), out_shape=(jax.ShapeD...  194 us
    pallas_call x1, Pallas kernels, shards(): pl.pallas_call(functools.partial(kernel, sizes), out_shape=(jax.ShapeDtyp...  145 us

profile of v1, /device:TPU:0, one launch (start us, length us, event | category | flops | bytes accessed | tf_op | source)
XLA Modules:
  0.0 342.5 jit_solution(7636111472406669589)
XLA Ops:
  0.6 193.6 %shard_map.68 = (bf16[2,384,4096]{2,1,0:T(8,128)(2,1)}, f32[2,2]{1,0:T(2,128)}, f32[2,3,32]{2,1,0:T(4,128)}) custom-call(s32[2]{0:T(128)} %live_ref.1, s32[2,32]{1,0:T(2,128)} %list_ref.1, bf16[384,6144]{1,0:T(8,128)(2,1)} %pool_hbm.1), custom_call_target="tpu_custom_call" | custom-call | tf_op jit(solution)/shard_map/pallas_call | solution.py:345
  194.2 144.6 %shard_map.69 = (bf16[2,384,512]{2,1,0:T(8,128)(2,1)}, f32[2,32,1024]{2,1,0:T(8,128)}) custom-call(f32[2,2]{1,0:T(2,128)} %get-tuple-element.7.live_ref, f32[2,3,32]{2,1,0:T(4,128)} %get-tuple-element.8.hit_ref, bf16[2,64,1024]{2,1,0:T(8,128)(2,1)} %factor_ref.1, bf16[2,256,1024]{2,1,0:T(8,128)(2,1)} %lower_ref.1, ...), custom_call_target="tpu_custom_call" | custom-call | tf_op jit(solution)/shard_map/pallas_call | solution.py:356
  338.8 2.1 copy.10
  340.9 1.7 copy.11

commit v2 on v1

--- a/solution.py
+++ b/solution.py
@@ -8,6 +8,8 @@
 from jax.sharding import PartitionSpec as P
 
 BLK = 128
+LAG = 8
+PAUSE = 2
 MESH = pl.DeviceIdType.MESH
 F32 = jnp.float32
 BF16 = jnp.bfloat16
@@ -188,12 +190,17 @@
     net = Net(send_sems, recv_sems)
     orders = ["xzy", "yzx", "zxy", "zyx"] if nx * ny > 1 else ["zxy"]
 
-    def gathers(make_view, rows):
-        count = min(len(orders), rows // 16)
-        step = rows // count
-        return [
-            gather(net, make_view(pl.ds(i * step, step)), orders[i], pos, sizes, peer) for i in range(count)
-        ]
+    def gathers(make_view, rows, flip=0):
+        unit = rows // 16
+        shares = [unit // 4] * 4
+        if unit == 16:
+            shares = [6, 5, 3, 2] if flip == 0 else [5, 6, 2, 3]
+        shares = shares[: len(orders)] if len(orders) > 1 else [unit]
+        tasks, start = [], 0
+        for order, share in zip(orders, shares):
+            tasks.append(gather(net, make_view(pl.ds(start, share * 16)), order, pos, sizes, peer))
+            start += share * 16
+        return tasks
 
     run(gathers(lambda rows: lambda zs, ys, xs: fbuf.at[:, zs, ys, xs, rows, :], piece_rows))
 
@@ -217,13 +224,15 @@
                 send_a[s, u, :, other] = part(1 - a, other).astype(BF16)
             sem = net.take(1)
             net.push(send_a.at[s, u], recv_a.at[s, u], sem, sem, peer(first))
-            yield
+            for _ in range(PAUSE if s == 0 else 1):
+                yield
             net.arrived(recv_a.at[s, u], sem, peer(first))
             send_b[s, u] = (part(a, 1 - b) + recv_a[s, u, :, 1 - b].astype(F32)).astype(BF16)
             sem = net.take(1)
             net.push(send_b.at[s, u], recv_b.at[s, u], sem, sem, peer(second))
             kept[s, u] = part(a, b) + recv_a[s, u, :, b].astype(F32)
-            yield
+            for _ in range(PAUSE if s == 0 else 1):
+                yield
             net.arrived(recv_b.at[s, u], sem, peer(second))
             kept[s, u] = kept[s, u] + recv_b[s, u].astype(F32)
         else:
@@ -233,7 +242,8 @@
         for d in range(1, nz):
             to = (z + d) % nz
             net.push(send_c.at[s, u, to], recv_c.at[s, u, d - 1], sem + d, sem + d, peer("z", to))
-        yield
+        for _ in range(PAUSE if s == 0 else 1):
+            yield
         total = kept[s, u, z]
         for d in range(1, nz):
             net.arrived(recv_c.at[s, u, d - 1], sem + d, peer("z", (z + d) % nz))
@@ -286,11 +296,11 @@
         yield from together([lower_half, scatter(s, 1)])
 
     def node(s):
-        for _ in range(4 * s):
+        for _ in range(LAG * s):
             yield
         scale(s)
         yield from together(
-            gathers(lambda rows: lambda zs, ys, xs: sbufs[s].at[zs, ys, xs, rows, :], slot_rows)
+            gathers(lambda rows: lambda zs, ys, xs: sbufs[s].at[zs, ys, xs, rows, :], slot_rows, s)
         )
         if s == 0:
             chosen_copy.wait()
@@ -300,35 +310,30 @@
     net.drain()
 
 
-def choose(slot_dev, live_ref, list_ref, pool_hbm, chosen_hbm, live_out, hit_out, sems):
+def choose(slot_dev, live_ref, list_ref, pool_ref, chosen_ref, live_out, hit_out):
     column = lax.axis_index("gcol")
     supernodes, own_blocks, slot_total = hit_out.shape
-    copies = []
     for s in range(supernodes):
         for j in range(slot_total):
-            block = list_ref[s, j]
-            copy = pltpu.make_async_copy(
-                pool_hbm.at[:, pl.ds(pl.multiple_of(block * BLK, BLK), BLK)],
-                chosen_hbm.at[s, :, pl.ds(j * BLK, BLK)],
-                sems.at[s, j],
-            )
-            copy.start()
-            copies.append(copy)
-    for s in range(supernodes):
-        live = live_ref[s]
-        for j in range(slot_dev):
-            live_out[s, j] = jnp.where(column * slot_dev + j < live, 1.0, 0.0)
-        for j in range(slot_total):
-            for b in range(own_blocks):
-                match = (list_ref[s, j] == column * own_blocks + b) & (j < live)
-                hit_out[s, b, j] = jnp.where(match, 1.0, 0.0)
-    for copy in copies:
-        copy.wait()
+            start = pl.multiple_of(list_ref[s, j] * BLK, BLK)
+            chosen_ref[s, :, j * BLK : (j + 1) * BLK] = pool_ref[:, pl.ds(start, BLK)]
+
+    @pl.when(pl.program_id(0) == 0)
+    def _():
+        for s in range(supernodes):
+            live = live_ref[s]
+            for j in range(slot_dev):
+                live_out[s, j] = jnp.where(column * slot_dev + j < live, 1.0, 0.0)
+            for j in range(slot_total):
+                for b in range(own_blocks):
+                    match = (list_ref[s, j] == column * own_blocks + b) & (j < live)
+                    hit_out[s, b, j] = jnp.where(match, 1.0, 0.0)
 
 
 def shards(ancestor_inverse, lower_rows, factor_inverse, block_lists, live_counts):
     supernodes, slot_rows, order_size = lower_rows.shape
-    own_rows = ancestor_inverse.shape[0]
+    own_rows, pool_width = ancestor_inverse.shape
+    step_rows = BLK // 2
     piece_rows = factor_inverse.shape[1]
     columns = lax.axis_size("gcol")
     side = 2 if lax.axis_size("groups") == 1 and columns % 4 == 0 else 1
@@ -349,9 +354,14 @@
             jax.ShapeDtypeStruct((supernodes, slot_dev), F32),
             jax.ShapeDtypeStruct((supernodes, own_rows // BLK, slot_total), F32),
         ),
-        in_specs=[smem, smem, pl.BlockSpec(memory_space=pl.ANY)],
-        out_specs=(pl.BlockSpec(memory_space=pl.ANY), smem, smem),
-        scratch_shapes=[pltpu.SemaphoreType.DMA((supernodes, slot_total))],
+        grid=(own_rows // step_rows,),
+        in_specs=[smem, smem, pl.BlockSpec((step_rows, pool_width), lambda i: (i, 0))],
+        out_specs=(
+            pl.BlockSpec((supernodes, step_rows, slot_total * BLK), lambda i: (0, i, 0)),
+            smem,
+            smem,
+        ),
+        compiler_params=pltpu.CompilerParams(vmem_limit_bytes=58 * 1024 * 1024),
     )(live_counts, block_lists, ancestor_inverse)
     ancestor, diagonal = pl.pallas_call(
         functools.partial(kernel, sizes),

time: 343 us -> 153 us (0.45)
  Pallas kernels: 338 us -> 148 us
    pallas_call x1, Pallas kernels: 194 us -> 7.27 us  [shards(): pl.pallas_call(functools.partial(choose, slot_dev), out_shape=(jax.ShapeD...]
    pallas_call x1, Pallas kernels: 145 us -> 141 us  [shards(): pl.pallas_call(functools.partial(kernel, sizes), out_shape=(jax.ShapeDtyp...]
where the time goes in v2:
time: 153 us
  Pallas kernels  148 us (97%)
  local copies, waits for them, and re-layouts  3.73 us (2%)
    pallas_call x1, Pallas kernels, shards(): pl.pallas_call(functools.partial(kernel, sizes), out_shape=(jax.ShapeDtyp...  141 us
    pallas_call x1, Pallas kernels, shards(): pl.pallas_call(functools.partial(choose, slot_dev), out_shape=(jax.ShapeD...  7.27 us
    unnamed x2, local copies, waits for them, and re-layouts  3.73 us

profile of v2, /device:TPU:0, one launch (start us, length us, event | category | flops | bytes accessed | tf_op | source)
XLA Modules:
  0.0 152.7 jit_solution(3943764416914166998)
XLA Ops:
  0.6 7.3 %shard_map.68 = (bf16[2,384,4096]{2,1,0:T(8,128)(2,1)}, f32[2,2]{1,0:T(2,128)}, f32[2,3,32]{2,1,0:T(4,128)}) custom-call(s32[2]{0:T(128)} %live_ref.1, s32[2,32]{1,0:T(2,128)} %list_ref.1, bf16[384,6144]{1,0:T(8,128)(2,1)} %pool_ref.1), custom_call_target="tpu_custom_call" | custom-call | tf_op jit(solution)/shard_map/pallas_call | solution.py:350
  7.9 141.1 %shard_map.69 = (bf16[2,384,512]{2,1,0:T(8,128)(2,1)}, f32[2,32,1024]{2,1,0:T(8,128)}) custom-call(f32[2,2]{1,0:T(2,128)} %get-tuple-element.7.live_ref, f32[2,3,32]{2,1,0:T(4,128)} %get-tuple-element.8.hit_ref, bf16[2,64,1024]{2,1,0:T(8,128)(2,1)} %factor_ref.1, bf16[2,256,1024]{2,1,0:T(8,128)(2,1)} %lower_ref.1, ...), custom_call_target="tpu_custom_call" | custom-call | tf_op jit(solution)/shard_map/pallas_call | solution.py:366
  149.0 2.1 %copy.10 = bf16[2,384,512]{2,1,0:T(8,128)(2,1)} copy(bf16[2,384,512]{2,1,0:T(8,128)(2,1)} %get-tuple-element.16) | data formatting | bytes 1572864
  151.0 1.7 %copy.11 = f32[2,1,32,1024]{3,2,1,0:T(8,128)} copy(f32[2,1,32,1024]{3,2,1,0:T(8,128)} %bitcast.3) | data formatting | bytes 524288

commit v3 on v2

--- a/solution.py
+++ b/solution.py
@@ -9,7 +9,8 @@
 
 BLK = 128
 LAG = 8
-PAUSE = 2
+CHUNKS = 2
+PAUSE = 3
 MESH = pl.DeviceIdType.MESH
 F32 = jnp.float32
 BF16 = jnp.bfloat16
@@ -211,43 +212,46 @@
             rows = slice(j * BLK, (j + 1) * BLK)
             sbufs[s][z, y, x, rows, :] = (product[rows] * live_ref[s, j]).astype(BF16)
 
-    def scatter(s, u):
+    def scatter(s, u, h):
+        width = half // CHUNKS
+        span = pl.ds(h * width, width)
         first, second = ("x", "y") if u == 0 else ("y", "x")
-        cols = own_cols if u == 0 else other_cols
+        side = parity if u == 0 else 1 - parity
+        cols = pl.ds(pl.multiple_of(side * half + h * width, width), width)
         if nx * ny > 1:
             def part(one, two):
                 index = {first: one, second: two}
-                return terms[s, u, :, index["y"], index["x"]]
+                return terms[s, u, :, index["y"], index["x"], :, span]
 
             a, b = pos[first], pos[second]
             for other in range(2):
-                send_a[s, u, :, other] = part(1 - a, other).astype(BF16)
+                send_a[s, u, h, :, other] = part(1 - a, other).astype(BF16)
             sem = net.take(1)
-            net.push(send_a.at[s, u], recv_a.at[s, u], sem, sem, peer(first))
+            net.push(send_a.at[s, u, h], recv_a.at[s, u, h], sem, sem, peer(first))
             for _ in range(PAUSE if s == 0 else 1):
                 yield
-            net.arrived(recv_a.at[s, u], sem, peer(first))
-            send_b[s, u] = (part(a, 1 - b) + recv_a[s, u, :, 1 - b].astype(F32)).astype(BF16)
+            net.arrived(recv_a.at[s, u, h], sem, peer(first))
+            send_b[s, u, h] = (part(a, 1 - b) + recv_a[s, u, h, :, 1 - b].astype(F32)).astype(BF16)
             sem = net.take(1)
-            net.push(send_b.at[s, u], recv_b.at[s, u], sem, sem, peer(second))
-            kept[s, u] = part(a, b) + recv_a[s, u, :, b].astype(F32)
+            net.push(send_b.at[s, u, h], recv_b.at[s, u, h], sem, sem, peer(second))
+            kept[s, u, h] = part(a, b) + recv_a[s, u, h, :, b].astype(F32)
             for _ in range(PAUSE if s == 0 else 1):
                 yield
-            net.arrived(recv_b.at[s, u], sem, peer(second))
-            kept[s, u] = kept[s, u] + recv_b[s, u].astype(F32)
+            net.arrived(recv_b.at[s, u, h], sem, peer(second))
+            kept[s, u, h] = kept[s, u, h] + recv_b[s, u, h].astype(F32)
         else:
-            kept[s, u] = terms[s, u, :, 0, 0]
-        send_c[s, u] = kept[s, u].astype(BF16)
+            kept[s, u, h] = terms[s, u, :, 0, 0, :, span]
+        send_c[s, u, h] = kept[s, u, h].astype(BF16)
         sem = net.take(nz)
         for d in range(1, nz):
             to = (z + d) % nz
-            net.push(send_c.at[s, u, to], recv_c.at[s, u, d - 1], sem + d, sem + d, peer("z", to))
+            net.push(send_c.at[s, u, h, to], recv_c.at[s, u, h, d - 1], sem + d, sem + d, peer("z", to))
         for _ in range(PAUSE if s == 0 else 1):
             yield
-        total = kept[s, u, z]
+        total = kept[s, u, h, z]
         for d in range(1, nz):
-            net.arrived(recv_c.at[s, u, d - 1], sem + d, peer("z", (z + d) % nz))
-            total = total + recv_c[s, u, d - 1].astype(F32)
+            net.arrived(recv_c.at[s, u, h, d - 1], sem + d, peer("z", (z + d) % nz))
+            total = total + recv_c[s, u, h, d - 1].astype(F32)
         diag_ref[s, :, cols] = total
 
     def finish(s):
@@ -288,12 +292,14 @@
             terms[s, u] = result.reshape(nz, ny, nx, out_rows, half)
 
         term(0, own_neg, own_cols)
-        lower_half = scatter(s, 0)
-        next(lower_half)
+        lower = [scatter(s, 0, h) for h in range(CHUNKS)]
+        for task in lower:
+            next(task)
         yield
         net.arrived(other_neg.at[s], sem, mate)
         term(1, other_neg, other_cols)
-        yield from together([lower_half, scatter(s, 1)])
+        upper = [scatter(s, 1, h) for h in range(CHUNKS)]
+        yield from together([task for pair in zip(lower, upper) for task in pair])
 
     def node(s):
         for _ in range(LAG * s):
@@ -333,7 +339,7 @@
 def shards(ancestor_inverse, lower_rows, factor_inverse, block_lists, live_counts):
     supernodes, slot_rows, order_size = lower_rows.shape
     own_rows, pool_width = ancestor_inverse.shape
-    step_rows = BLK // 2
+    step_rows = BLK
     piece_rows = factor_inverse.shape[1]
     columns = lax.axis_size("gcol")
     side = 2 if lax.axis_size("groups") == 1 and columns % 4 == 0 else 1
@@ -342,7 +348,7 @@
     half = order_size // lax.axis_size("grow")
     out_rows = half // columns
     grid = (nz, side, side)
-    sems = (1 + supernodes) * (4 if side > 1 else 1) * (4 * nz + 2) + supernodes * (1 + 2 * (2 + nz))
+    sems = 2 * supernodes * (4 if side > 1 else 1) * (4 * nz + 2) + supernodes * (1 + 2 * CHUNKS * (2 + nz))
     slot_total = block_lists.shape[1]
     slot_dev = slot_rows // BLK
     chosen_shape = (supernodes, own_rows, slot_total * BLK)
@@ -386,13 +392,13 @@
             pltpu.VMEM((supernodes, own_rows, half), BF16),
             pltpu.VMEM((supernodes, own_rows, half), BF16),
             pltpu.VMEM((supernodes, 2) + grid + (out_rows, half), F32),
-            pltpu.VMEM((supernodes, 2, nz, out_rows, half), F32),
-            pltpu.VMEM((supernodes, 2, nz, side, out_rows, half), BF16),
-            pltpu.VMEM((supernodes, 2, nz, side, out_rows, half), BF16),
-            pltpu.VMEM((supernodes, 2, nz, out_rows, half), BF16),
-            pltpu.VMEM((supernodes, 2, nz, out_rows, half), BF16),
-            pltpu.VMEM((supernodes, 2, nz, out_rows, half), BF16),
-            pltpu.VMEM((supernodes, 2, nz, out_rows, half), BF16),
+            pltpu.VMEM((supernodes, 2, CHUNKS, nz, out_rows, half // CHUNKS), F32),
+            pltpu.VMEM((supernodes, 2, CHUNKS, nz, side, out_rows, half // CHUNKS), BF16),
+            pltpu.VMEM((supernodes, 2, CHUNKS, nz, side, out_rows, half // CHUNKS), BF16),
+            pltpu.VMEM((supernodes, 2, CHUNKS, nz, out_rows, half // CHUNKS), BF16),
+            pltpu.VMEM((supernodes, 2, CHUNKS, nz, out_rows, half // CHUNKS), BF16),
+            pltpu.VMEM((supernodes, 2, CHUNKS, nz, out_rows, half // CHUNKS), BF16),
+            pltpu.VMEM((supernodes, 2, CHUNKS, nz, out_rows, half // CHUNKS), BF16),
             pltpu.SemaphoreType.DMA((sems,)),
             pltpu.SemaphoreType.DMA((sems,)),
             pltpu.SemaphoreType.DMA,

time: 153 us -> 150 us (0.980)
  Pallas kernels: 148 us -> 146 us
    pallas_call x1, Pallas kernels: 141 us -> 139 us  [shards(): pl.pallas_call(functools.partial(kernel, sizes), out_shape=(jax.ShapeDtyp...]
where the time goes in v3:
time: 150 us
  Pallas kernels  146 us (97%)
  local copies, waits for them, and re-layouts  3.73 us (2%)
    pallas_call x1, Pallas kernels, shards(): pl.pallas_call(functools.partial(kernel, sizes), out_shape=(jax.ShapeDtyp...  139 us
    pallas_call x1, Pallas kernels, shards(): pl.pallas_call(functools.partial(choose, slot_dev), out_shape=(jax.ShapeD...  6.79 us
    unnamed x2, local copies, waits for them, and re-layouts  3.73 us

profile of v3, /device:TPU:0, one launch (start us, length us, event | category | flops | bytes accessed | tf_op | source)
XLA Modules:
  0.0 150.0 jit_solution(9736439516502278122)
XLA Ops:
  0.6 6.8 %shard_map.68 = (bf16[2,384,4096]{2,1,0:T(8,128)(2,1)}, f32[2,2]{1,0:T(2,128)}, f32[2,3,32]{2,1,0:T(4,128)}) custom-call(s32[2]{0:T(128)} %live_ref.1, s32[2,32]{1,0:T(2,128)} %list_ref.1, bf16[384,6144]{1,0:T(8,128)(2,1)} %pool_ref.1), custom_call_target="tpu_custom_call" | custom-call | tf_op jit(solution)/shard_map/pallas_call | solution.py:356
  7.4 138.8 %shard_map.69 = (bf16[2,384,512]{2,1,0:T(8,128)(2,1)}, f32[2,32,1024]{2,1,0:T(8,128)}) custom-call(f32[2,2]{1,0:T(2,128)} %get-tuple-element.7.live_ref, f32[2,3,32]{2,1,0:T(4,128)} %get-tuple-element.8.hit_ref, bf16[2,64,1024]{2,1,0:T(8,128)(2,1)} %factor_ref.1, bf16[2,256,1024]{2,1,0:T(8,128)(2,1)} %lower_ref.1, ...), custom_call_target="tpu_custom_call" | custom-call | tf_op jit(solution)/shard_map/pallas_call | solution.py:372
  146.3 2.1 %copy.10 = bf16[2,384,512]{2,1,0:T(8,128)(2,1)} copy(bf16[2,384,512]{2,1,0:T(8,128)(2,1)} %get-tuple-element.16) | data formatting | bytes 1572864
  148.3 1.7 %copy.11 = f32[2,1,32,1024]{3,2,1,0:T(8,128)} copy(f32[2,1,32,1024]{3,2,1,0:T(8,128)} %bitcast.3) | data formatting | bytes 524288
